TPU v7x, 32 devices: a whole 2x2x4 slice. The times are simulated.
32 devices in a mesh: expert: 8 (over y, x, core), tensor: 4 (over z).
Axes of the slice: x: 2, y: 2, z: 4, core: 2. Of those that a mesh axis runs over, the one named last changes fastest.
Arguments:
- tokens: bfloat16 [1024, 4096], P('expert', 'tensor'), may hold values from -6 to 6
- routes: int32 [1024, 2], P('expert'), may hold values from 0 to 7, all different within a row; in each aligned block of 128 rows (0 to 127, 128 to 255, ...) at most 64 rows name the same one
- route_gates: float32 [1024, 2], P('expert'), may hold values from 0.1 to 0.6
- gate_weight: bfloat16 [8, 4096, 2048], P('expert', None, 'tensor'), may hold values from -0.09375 to 0.09375
- up_weight: bfloat16 [8, 4096, 2048], P('expert', None, 'tensor'), may hold values from -0.09375 to 0.09375
- down_weight: bfloat16 [8, 2048, 4096], P('expert', 'tensor'), may hold values from -0.1875 to 0.1875
Outputs:
- combined: bfloat16 [1024, 4096], P('expert', 'tensor')
Inputs may be any that keep to these rules, and one draw needn't show every extreme that they name: Within each aligned block of 128 tokens no expert is named by more than 64 routes, and the 2 experts of one token differ.
All inputs are finite; a program needn't handle non-finite values.
Results may differ from a plain program's by a relative error of at most 0.02.
Values may be sent and summed in bfloat16 or wider, within the bound.
No kernel may reach another device: no remote copies, remote signals or barrier semaphores. Data moves between devices by JAX's collectives and lax.ppermute only.
A program may use at most 64 MiB of HBM per device.

v0:
```python
import jax
import jax.numpy as jnp
from jax import lax
from jax.sharding import PartitionSpec as P


def shards(tokens, routes, route_gates, gate_weight, up_weight, down_weight):
    token_count = tokens.shape[0]
    slice_width = tokens.shape[1]
    route_count = routes.shape[1]
    source_count = lax.axis_size("expert")
    expert_count = gate_weight.shape[0] * source_count
    capacity = 2 * token_count * route_count // expert_count
    slot_total = source_count * capacity
    flat_routes = routes.reshape(-1)
    onehot = (flat_routes[:, None] == jnp.arange(expert_count, dtype=jnp.int32)[None, :]).astype(
        jnp.int32
    )
    before = jnp.cumsum(onehot, axis=0) - onehot
    slot_ids = jnp.sum(before * onehot, axis=1)
    places = flat_routes * capacity + slot_ids
    token_ids = jnp.arange(token_count * route_count, dtype=jnp.int32) // route_count
    outgoing = (
        jnp.zeros((expert_count * capacity, slice_width), jnp.bfloat16)
        .at[places]
        .set(tokens[token_ids])
    )
    outgoing = outgoing.reshape(expert_count, capacity, slice_width)
    arrived = lax.all_to_all(outgoing, "expert", split_axis=0, concat_axis=0, tiled=True)
    received = arrived.reshape(slot_total, slice_width)
    gate_local = gate_weight[0]
    up_local = up_weight[0]
    down_local = down_weight[0]
    segment = lax.all_gather(received, "tensor", axis=1, tiled=True)
    gate_proj = jnp.dot(segment, gate_local, preferred_element_type=jnp.float32)
    up_proj = jnp.dot(segment, up_local, preferred_element_type=jnp.float32)
    hidden = (jax.nn.silu(gate_proj) * up_proj).astype(jnp.bfloat16)
    partial_value = lax.dot_general(
        down_local, hidden, (((0,), (1,)), ((), ())), preferred_element_type=jnp.float32
    )
    summed = lax.psum_scatter(
        partial_value.astype(jnp.bfloat16).astype(jnp.float32).astype(jnp.bfloat16),
        "tensor",
        scatter_dimension=0,
        tiled=True,
    )
    expert_out = summed.reshape(slice_width, source_count, capacity)
    returned = lax.all_to_all(expert_out, "expert", split_axis=1, concat_axis=1, tiled=True)
    flat_back = returned.reshape(slice_width, expert_count * capacity)
    picked = jnp.take(flat_back, places, axis=1).astype(jnp.float32)
    weighted = picked * route_gates.reshape(-1)[None, :]
    combined = jnp.sum(weighted.reshape(slice_width, token_count, route_count), axis=2)
    return combined.T.astype(jnp.bfloat16)


def solution(mesh):
    return jax.shard_map(
        shards,
        mesh=mesh,
        in_specs=(
            P("expert", "tensor"),
            P("expert", None),
            P("expert", None),
            P("expert", None, "tensor"),
            P("expert", None, "tensor"),
            P("expert", "tensor", None),
        ),
        out_specs=P("expert", "tensor"),
        check_vma=False,
    )
```

profile of v0, /device:TPU:0, one launch (start us, length us, event | category | flops | bytes accessed | tf_op | source)
XLA Modules:
  0.0 231.8 jit_solution(11133696388727786495)
XLA Ops:
  6.5 0.0 copy-start
  6.5 0.0 all-gather.2.cloned.1.call-start
  6.5 0.8 copy.13
  7.4 0.1 eq.26
  7.5 0.1 reshape.123
  7.6 0.7 broadcast_multiply_fusion
  8.4 0.6 reduce-window.6
  8.9 0.2 slice_reduce_fusion
  9.2 0.1 copy.17
  9.3 0.1 mul.41
  9.5 0.1 fusion.16
  9.6 0.0 copy-done
  9.6 3.7 %scatter_custom_fusion = bf16[512,1024]{1,0:T(8,128)(2,1)S(1)} fusion(s32[256]{0:T(256)S(1)} %bitcast.45, bf16[128,1024]{1,0:T(8,128)(2,1)S(1)} %copy-done, s32[1024]{0:T(1024)S(1)} %pad_clamp_fusion.1, bf16[]{:T(256)} %constant.42.clone.1), kind=kCustom, calls=%fused_computation.14 | custom fusion | bytes 1048578 | tf_op jit(solution)/shard_map/scatter | solution.py:26
  13.3 20.4 %all_to_all.10 = bf16[8,64,1024]{2,1,0:T(8,128)(2,1)} all-to-all(bf16[8,64,1024]{2,1,0:T(8,128)(2,1)S(1)} %bitcast.41), channel_id=1, replica_groups=mesh['expert'=8,'tensor'=4] {'expert'}, dimensions={0} | all-to-all | bytes 2097152 | tf_op jit(solution)/shard_map/all_to_all | solution.py:29
  33.7 0.0 all-gather.2.cloned.1.call-update
  33.8 0.0 reduce-scatter.2.cloned.1.call-start
  33.8 80.2 %all-gather.2.cloned.1.call-done = bf16[512,4096]{1,0:T(8,128)(2,1)} async-done(((bf16[512,1024]{1,0:T(8,128)(2,1)}), bf16[512,4096]{1,0:T(8,128)(2,1)}) %all-gather.2.cloned.1.call-update) | async-done | bytes 4194320 | tf_op jit(solution)/shard_map/all_gather | solution.py:34
  114.0 0.0 copy-start.3
  114.0 0.0 copy-start.5
  114.0 5.9 %fusion.4 = f32[512,512]{1,0:T(8,128)S(1)} fusion(bf16[512,4096]{1,0:T(8,128)(2,1)} %all-gather.2.cloned.1.call-done, bf16[1,4096,512]{2,1,0:T(8,128)(2,1)} %param.9), kind=kOutput, calls=%fused_computation.8 | convolution fusion | flops 2147483648 | bytes 9437184 | tf_op jit(solution)/shard_map/dot_general | solution.py:35
  120.0 0.0 copy-done.3
  120.0 0.0 copy-done.5
  120.0 0.0 copy-start.4
  120.0 2.4 %fusion.9 = bf16[512,512]{1,0:T(8,128)(2,1)S(1)} fusion(bf16[512,4096]{1,0:T(8,128)(2,1)S(1)} %copy-done.5, bf16[1,4096,512]{2,1,0:T(8,128)(2,1)S(1)} %copy-done.3, f32[512,512]{1,0:T(8,128)S(1)} %fusion.4), kind=kOutput, calls=%fused_computation.11 | convolution fusion | flops 2149056512 | bytes 9961472 | tf_op jit(solution)/shard_map/dot_general | solution.py:36
  122.5 0.0 copy-done.4
  122.5 4.3 %fusion = bf16[4096,512]{0,1:T(8,128)(2,1)} fusion(bf16[512,512]{1,0:T(8,128)(2,1)S(1)} %fusion.9, bf16[1,512,4096]{2,1,0:T(8,128)(2,1)S(1)} %copy-done.4), kind=kOutput, calls=%fused_computation.4 | convolution fusion | flops 2149580800 | bytes 8912896 | tf_op jit(solution)/shard_map/dot_general | solution.py:38
  126.7 0.0 copy-start.1
  126.7 0.0 copy-start.2
  126.7 0.0 reduce-scatter.2.cloned.1.call-update
  126.8 75.4 %reduce-scatter.2.cloned.1.call-done = bf16[1024,512]{0,1:T(8,128)(2,1)} async-done(((bf16[4096,512]{0,1:T(8,128)(2,1)}), bf16[1024,512]{0,1:T(8,128)(2,1)}) %reduce-scatter.2.cloned.1.call-update) | async-done | bytes 1048592 | tf_op jit(solution)/shard_map/reduce_scatter | solution.py:41
  202.2 3.7 %all-to-all-start.1 = ((bf16[1024,8,64]{0,2,1:T(8,128)(2,1)}), bf16[1024,8,64]{0,2,1:T(8,128)(2,1)S(1)}, u32[]{:S(2)}, u32[]{:S(2)}) async-start(bf16[1024,8,64]{0,2,1:T(8,128)(2,1)} %bitcast.43), calls=%async_computation.2 | async-start | bytes 2097152 | tf_op jit(solution)/shard_map/all_to_all | solution.py:48
  205.9 0.1 reduce_sum.23
  206.1 0.1 copy.15
  206.2 0.0 copy-done.1
  206.2 0.1 copy.16
  206.3 0.0 copy-done.2
  206.3 0.1 copy.18
  206.5 14.8 %all-to-all-done.1 = bf16[1024,8,64]{0,2,1:T(8,128)(2,1)S(1)} async-done(((bf16[1024,8,64]{0,2,1:T(8,128)(2,1)}), bf16[1024,8,64]{0,2,1:T(8,128)(2,1)S(1)}, u32[]{:S(2)}, u32[]{:S(2)}) %all-to-all-start.1) | async-done | bytes 1048608 | tf_op jit(solution)/shard_map/all_to_all | solution.py:48
  221.3 1.2 gather_fusion
  222.4 0.2 gather.11
  222.7 2.3 %multiply_reduce_fusion = bf16[1024,128]{0,1:T(8,128)(2,1)} fusion(bf16[1024,128,2]{0,2,1:T(2,128)(2,1)S(1)} %gather.11, pred[128,2]{1,0:T(8,128)(4,1)S(1)} %copy.16, f32[128,2]{1,0:T(8,128)S(1)} %copy.18), kind=kLoop, calls=%fused_computation.12 | loop fusion | flops 917504 | bytes 787712 | tf_op jit(solution)/shard_map/reduce_sum | solution.py:52
  (8 shorter events, 0.1 us)
Async XLA Ops:
  6.5 3.0 %copy-start = (bf16[128,1024]{1,0:T(8,128)(2,1)S(1)}, bf16[128,1024]{1,0:T(8,128)(2,1)}, u32[]{:S(2)}) copy-start(bf16[128,1024]{1,0:T(8,128)(2,1)} %param.6) | copy-start | bytes 786436
  6.5 107.5 %all-gather.2.cloned.1.call-start = ((), (), s32[]{:S(2)}) async-start(), calls=%async_computation.3 | async-start | bytes 5242880 | tf_op jit(solution)/shard_map/all_gather | solution.py:34
  33.8 168.4 %reduce-scatter.2.cloned.1.call-start = ((), (), s32[]{:S(2)}) async-start(), calls=%async_computation.4 | async-start | bytes 5242880 | tf_op jit(solution)/shard_map/reduce_scatter | solution.py:41
  114.0 5.9 %copy-start.3 = (bf16[1,4096,512]{2,1,0:T(8,128)(2,1)S(1)}, bf16[1,4096,512]{2,1,0:T(8,128)(2,1)}, u32[]{:S(2)}) copy-start(bf16[1,4096,512]{2,1,0:T(8,128)(2,1)} %param.10) | copy-start | bytes 12582916
  114.0 5.9 %copy-start.5 = (bf16[512,4096]{1,0:T(8,128)(2,1)S(1)}, bf16[512,4096]{1,0:T(8,128)(2,1)}, u32[]{:S(2)}) copy-start(bf16[512,4096]{1,0:T(8,128)(2,1)} %all-gather.2.cloned.1.call-done) | copy-start | bytes 12582916
  120.0 2.5 %copy-start.4 = (bf16[1,512,4096]{2,1,0:T(8,128)(2,1)S(1)}, bf16[1,512,4096]{2,1,0:T(8,128)(2,1)}, u32[]{:S(2)}) copy-start(bf16[1,512,4096]{2,1,0:T(8,128)(2,1)} %param.11) | copy-start | bytes 12582916
  126.7 79.4 %copy-start.1 = (s32[128,2]{0,1:T(2,128)S(1)}, s32[128,2]{0,1:T(2,128)}, u32[]{:S(2)}) copy-start(s32[128,2]{0,1:T(2,128)} %param.7) | copy-start | bytes 3076
  126.7 79.6 %copy-start.2 = (f32[128,2]{0,1:T(2,128)S(1)}, f32[128,2]{0,1:T(2,128)}, u32[]{:S(2)}) copy-start(f32[128,2]{0,1:T(2,128)} %param.8) | copy-start | bytes 3076
  202.2 19.1 %all-to-all-start.1 = ((bf16[1024,8,64]{0,2,1:T(8,128)(2,1)}), bf16[1024,8,64]{0,2,1:T(8,128)(2,1)S(1)}, u32[]{:S(2)}, u32[]{:S(2)}) async-start(bf16[1024,8,64]{0,2,1:T(8,128)(2,1)} %bitcast.43), calls=%async_computation.2 | async-start | bytes 2097152 | tf_op jit(solution)/shard_map/all_to_all | solution.py:48
Sparse Core Ops, SparseCore 0:
  33.9 80.1 all-gather.1
  126.9 75.2 reduce-scatter.1
where the time goes:
time: 232 us
  waiting for transfers between devices  171 us (74%)
  blocking collectives  20.4 us (9%)
  between operations  13.5 us (6%)
  matrix products  12.6 us (5%)
  local copies, waits for them, and re-layouts  7.12 us (3%)
  other arithmetic  3.8 us (2%)
  starting transfers between devices  3.78 us (2%)
    all_gather x1, waiting for transfers between devices, shards(): segment = lax.all_gather(received, 'tensor', axis=1, tiled=True)  80.2 us
    reduce_scatter x1, waiting for transfers between devices, shards(): lax.psum_scatter(partial_value.astype(jnp.bfloat16).astype(jnp.float32).a...  75.4 us
    all_to_all x1, blocking collectives, shards(): lax.all_to_all(outgoing, 'expert', split_axis=0, concat_axis=0, tiled=True)  20.4 us
    all_to_all x1, waiting for transfers between devices, shards(): lax.all_to_all(expert_out, 'expert', split_axis=1, concat_axis=1, tiled=T...  14.8 us
    dot_general x1, matrix products, shards(): gate_proj = jnp.dot(segment, gate_local, preferred_element_type=jnp.float32)  5.92 us
  transfers between devices with their start and end apart: 3, of which 3 were waited for; matrix products, arithmetic and copies ran while one was open for 0% of the time, Pallas kernels for 0%

commit v1 on v0

--- a/solution.py
+++ b/solution.py
@@ -1,10 +1,16 @@
+import functools
+
 import jax
 import jax.numpy as jnp
 from jax import lax
+from jax.experimental import pallas as pl
+from jax.experimental.pallas import tpu as pltpu
 from jax.sharding import PartitionSpec as P
 
-
-def shards(tokens, routes, route_gates, gate_weight, up_weight, down_weight):
+VMEM_BYTES = 40 * 1024 * 1024
+
+
+def dispatch_plan(tokens, routes, route_gates, gate_weight, up_weight, down_weight):
     token_count = tokens.shape[0]
     slice_width = tokens.shape[1]
     route_count = routes.shape[1]
@@ -28,21 +34,15 @@
     outgoing = outgoing.reshape(expert_count, capacity, slice_width)
     arrived = lax.all_to_all(outgoing, "expert", split_axis=0, concat_axis=0, tiled=True)
     received = arrived.reshape(slot_total, slice_width)
-    gate_local = gate_weight[0]
-    up_local = up_weight[0]
-    down_local = down_weight[0]
     segment = lax.all_gather(received, "tensor", axis=1, tiled=True)
-    gate_proj = jnp.dot(segment, gate_local, preferred_element_type=jnp.float32)
-    up_proj = jnp.dot(segment, up_local, preferred_element_type=jnp.float32)
+    gate_proj = jnp.dot(segment, gate_weight[0], preferred_element_type=jnp.float32)
+    up_proj = jnp.dot(segment, up_weight[0], preferred_element_type=jnp.float32)
     hidden = (jax.nn.silu(gate_proj) * up_proj).astype(jnp.bfloat16)
     partial_value = lax.dot_general(
-        down_local, hidden, (((0,), (1,)), ((), ())), preferred_element_type=jnp.float32
+        down_weight[0], hidden, (((0,), (1,)), ((), ())), preferred_element_type=jnp.float32
     )
     summed = lax.psum_scatter(
-        partial_value.astype(jnp.bfloat16).astype(jnp.float32).astype(jnp.bfloat16),
-        "tensor",
-        scatter_dimension=0,
-        tiled=True,
+        partial_value.astype(jnp.bfloat16), "tensor", scatter_dimension=0, tiled=True
     )
     expert_out = summed.reshape(slice_width, source_count, capacity)
     returned = lax.all_to_all(expert_out, "expert", split_axis=1, concat_axis=1, tiled=True)
@@ -53,9 +53,215 @@
     return combined.T.astype(jnp.bfloat16)
 
 
+def arrival(step):
+    return step ^ (step >> 1)
+
+
+def ffn_kernel(
+    groups, blocks, splits, separate, place_ref, *refs
+):
+    x_refs = refs[: blocks * groups]
+    coef_ref, gate0, up0, gate1, up1, down0, down1 = refs[blocks * groups : blocks * groups + 7]
+    out_count = blocks if separate else groups
+    out_refs = refs[blocks * groups + 7 : blocks * groups + 7 + out_count]
+    x_all, totals, hidden, sems = refs[blocks * groups + 7 + out_count :]
+    rows = x_refs[0].shape[0]
+    depth = gate0.shape[0]
+    half = gate0.shape[1]
+    step = pl.program_id(0)
+    inner = blocks * splits
+
+    def copy(block, group):
+        return pltpu.make_async_copy(
+            x_refs[block * groups + group],
+            x_all.at[block, pl.ds(group * rows, rows), :],
+            sems.at[block, group],
+        )
+
+    @pl.when(step == 0)
+    def _():
+        for block in range(blocks):
+            for group in range(groups):
+                copy(block, group).start()
+        totals[...] = jnp.zeros_like(totals)
+
+    for block in range(blocks):
+
+        @pl.when(step == block * splits)
+        def _():
+            for group in range(groups):
+                copy(block, group).wait()
+
+    @pl.when(step < inner)
+    def _():
+        columns = pl.ds(pl.multiple_of(lax.rem(step, splits) * depth, depth), depth)
+        x = x_all[lax.div(step, splits), :, columns]
+        for place, weight in enumerate((gate0, up0, gate1, up1)):
+            totals[place] += jnp.dot(x, weight[...], preferred_element_type=jnp.float32)
+
+    @pl.when(step == inner - 1)
+    def _():
+        for expert in range(2):
+            gate = totals[2 * expert]
+            value = gate / (1.0 + jnp.exp(-gate)) * totals[2 * expert + 1]
+            hidden[:, expert * half : (expert + 1) * half] = (
+                value * coef_ref[:, expert : expert + 1]
+            ).astype(jnp.bfloat16)
+
+    @pl.when(step >= inner)
+    def _():
+        part = jnp.dot(hidden[:, :half], down0[...], preferred_element_type=jnp.float32)
+        part += jnp.dot(hidden[:, half:], down1[...], preferred_element_type=jnp.float32)
+        part = part.astype(jnp.bfloat16)
+        if separate:
+            for block in range(blocks):
+
+                @pl.when(step == inner + block)
+                def _():
+                    out_refs[block][...] = part
+        else:
+            for group in range(groups):
+                out_refs[group][0] = part[group * rows : (group + 1) * rows]
+
+
+def ffn(place, xs, coef, weights, separate):
+    blocks, groups = len(xs), len(xs[0])
+    rows, width = xs[0][0].shape
+    half = weights[0].shape[1]
+    splits = 2 if width % 256 == 0 else 1
+    depth = width // splits
+    inner = blocks * splits
+
+    def into(step, place):
+        now = jnp.minimum(step, inner - 1)
+        source = lax.rem(place[0] - arrival(now // splits) + blocks, blocks)
+        return source * splits + lax.rem(now, splits), 0
+
+    def leaving(step):
+        return jnp.maximum(step - inner, 0)
+
+    def out_of(step, place):
+        return 0, lax.rem(place[0] + arrival(blocks - 1 - leaving(step)), blocks)
+
+    whole = lambda step, place: (0, 0)
+    if separate:
+        out_shape = [jax.ShapeDtypeStruct((groups * rows, width), jnp.bfloat16)] * blocks
+        out_specs = [pl.BlockSpec((groups * rows, width), whole)] * blocks
+    else:
+        out_shape = [jax.ShapeDtypeStruct((blocks, rows, width), jnp.bfloat16)] * groups
+        out_specs = [
+            pl.BlockSpec((1, rows, width), lambda step, place: (leaving(step), 0, 0))
+        ] * groups
+    total_rows = groups * rows
+    return pl.pallas_call(
+        functools.partial(ffn_kernel, groups, blocks, splits, separate),
+        out_shape=out_shape,
+        grid_spec=pltpu.PrefetchScalarGridSpec(
+            num_scalar_prefetch=1,
+            grid=(inner + blocks,),
+            in_specs=[pl.BlockSpec(memory_space=pl.ANY)] * (blocks * groups)
+            + [pl.BlockSpec((total_rows, 2), whole)]
+            + [pl.BlockSpec((depth, half), into)] * 4
+            + [pl.BlockSpec((half, width), out_of)] * 2,
+            out_specs=out_specs,
+            scratch_shapes=[
+                pltpu.VMEM((blocks, total_rows, width), jnp.bfloat16),
+                pltpu.VMEM((4, total_rows, half), jnp.float32),
+                pltpu.VMEM((total_rows, 2 * half), jnp.bfloat16),
+                pltpu.SemaphoreType.DMA((blocks, groups)),
+            ],
+        ),
+        compiler_params=pltpu.CompilerParams(vmem_limit_bytes=VMEM_BYTES),
+        cost_estimate=pl.CostEstimate(
+            flops=2 * total_rows * blocks * width * 6 * half,
+            bytes_accessed=12 * blocks * width * half + 4 * blocks * total_rows * width,
+            transcendentals=total_rows * 2 * half,
+        ),
+    )(place, *[x for block in xs for x in block], coef, *weights)
+
+
+def after(value, *earlier):
+    return lax.optimization_barrier((value,) + earlier)[0]
+
+
+def gather_plan(tokens, routes, route_gates, gate_weight, up_weight, down_weight):
+    devices = lax.axis_size("expert")
+    depth = lax.axis_size("tensor")
+    me = lax.axis_index("expert")
+    place = lax.axis_index("tensor")
+    wide = jnp.float32
+    narrow = jnp.bfloat16
+
+    def over(value, which):
+        pairs = [(i, i ^ ((2, 4) if i % 2 == which else (4, 2))[0]) for i in range(devices)]
+        return lax.ppermute(value, "expert", pairs)
+
+    def near(value):
+        return over(value, 0)
+
+    def far(value):
+        return over(value, 1)
+
+    def twin(value):
+        return lax.ppermute(value, "expert", [(i, i ^ 1) for i in range(devices)])
+
+    def shift(value, by):
+        return lax.ppermute(value, "tensor", [(i, (i + by) % depth) for i in range(depth)])
+
+    named = routes[:, :, None] == jnp.arange(devices, dtype=jnp.int32)[None, None, :]
+    coef = jnp.sum(jnp.where(named, route_gates[:, :, None], 0.0), axis=1)
+
+    order = [arrival(i) for i in range(depth)]
+    own = [tokens if by == 0 else shift(tokens, by) for by in order]
+    a, b, g = [], [], []
+    coef_a, coef_b = near(coef), far(coef)
+    coef_g = near(coef_b)
+    for block in own:
+        a.append(near(block))
+        b.append(far(block))
+        g.append(near(b[-1]))
+
+    mine = [gate_weight[0], up_weight[0], down_weight[0]]
+    other = [twin(w) for w in mine]
+    weights = [mine[0], mine[1], other[0], other[1], mine[2], other[2]]
+    place = place.astype(jnp.int32).reshape(1)
+
+    def gates_of(value):
+        return jnp.concatenate(
+            [
+                lax.dynamic_slice_in_dim(value, me, 1, axis=1),
+                lax.dynamic_slice_in_dim(value, me ^ 1, 1, axis=1),
+            ],
+            axis=1,
+        )
+
+    coef_main = gates_of(jnp.concatenate([coef, coef_a, coef_b], axis=0))
+    main = [[own[i], a[i], b[i]] for i in range(depth)]
+    y_own, y_a, y_b = ffn(place, main, coef_main, weights, False)
+    y_g = ffn(place, [[v] for v in g], gates_of(coef_g), weights, True)
+
+    from_a = near(y_a)
+    result = None
+    arrived = []
+    for i in range(depth):
+        by = order[depth - 1 - i]
+        passed = near(y_g[i])
+        send = (y_b[i].astype(wide) + passed.astype(wide)).astype(narrow)
+        from_b = far(send)
+        total = y_own[i].astype(wide) + from_a[i].astype(wide) + from_b.astype(wide)
+        if by == 0:
+            result = total
+        else:
+            arrived.append(shift(total.astype(narrow), by))
+    for value in arrived:
+        result = result + value.astype(wide)
+    return result.astype(narrow)
+
+
 def solution(mesh):
+    small = mesh.shape["expert"] == 8 and mesh.shape["tensor"] == 4
     return jax.shard_map(
-        shards,
+        gather_plan if small else dispatch_plan,
         mesh=mesh,
         in_specs=(
             P("expert", "tensor"),

time: 232 us -> 155 us (0.67)
  waiting for transfers between devices: 171 us -> 64.3 us
  starting transfers between devices: 3.78 us -> 47.6 us
  Pallas kernels: 0 us -> 31 us
  blocking collectives: 20.4 us -> 0 us
  between operations: 13.5 us -> 0.13 us
  matrix products: 12.6 us -> 0 us
    all_gather x1 -> x0, waiting for transfers between devices: 80.2 us -> none  [shards(): segment = lax.all_gather(received, 'tensor', axis=1, tiled=True)]
    reduce_scatter x1 -> x0, waiting for transfers between devices: 75.4 us -> none  [shards(): lax.psum_scatter(partial_value.astype(jnp.bfloat16).astype(jnp.float32).a...]
    ppermute x0 -> x33, waiting for transfers between devices: none -> 64.3 us  [the longest x24 47.4 us: over(): return lax.ppermute(value, 'expert', pairs)]
    ppermute x0 -> x33, starting transfers between devices: none -> 47.6 us  [the longest x24 28.6 us: over(): return lax.ppermute(value, 'expert', pairs)]
    pallas_call x0 -> x2, Pallas kernels: none -> 31 us  [ffn(): pl.pallas_call(functools.partial(ffn_kernel, groups, blocks, splits, sepa...]
    all_to_all x1 -> x0, blocking collectives: 20.4 us -> none  [shards(): lax.all_to_all(outgoing, 'expert', split_axis=0, concat_axis=0, tiled=True)]
    all_to_all x1 -> x0, waiting for transfers between devices: 14.8 us -> none  [shards(): lax.all_to_all(expert_out, 'expert', split_axis=1, concat_axis=1, tiled=T...]
    dot_general x3 -> x0, matrix products: 12.6 us -> none  [the longest x1 5.92 us: shards(): gate_proj = jnp.dot(segment, gate_local, preferred_element_type=jnp.float32)]
  transfers between devices with their start and end apart: 3 -> 33, of which waited for: 3 -> 21; matrix products, arithmetic and copies ran while one was open for 0% -> 1% of each run, Pallas kernels for 0% -> 20%
where the time goes in v1:
time: 155 us; the launch traced here: 154 us
  waiting for transfers between devices  64.3 us (41%)
  starting transfers between devices  47.6 us (31%)
  Pallas kernels  31 us (20%)
  local copies, waits for them, and re-layouts  8.39 us (5%)
  other arithmetic  2.55 us (2%)
    ppermute x24, waiting for transfers between devices, over(): return lax.ppermute(value, 'expert', pairs)  47.4 us
    pallas_call x2, Pallas kernels, ffn(): pl.pallas_call(functools.partial(ffn_kernel, groups, blocks, splits, sepa...  31 us
    ppermute x24, starting transfers between devices, over(): return lax.ppermute(value, 'expert', pairs)  28.6 us
    ppermute x6, starting transfers between devices, shift(): lax.ppermute(value, 'tensor', [(i, (i + by) % depth) for i in range(depth)])  18 us
    ppermute x6, waiting for transfers between devices, shift(): lax.ppermute(value, 'tensor', [(i, (i + by) % depth) for i in range(depth)])  16.9 us
    unnamed x20, local copies, waits for them, and re-layouts  8.12 us
  transfers between devices with their start and end apart: 33, of which 21 were waited for; matrix products, arithmetic and copies ran while one was open for 1% of the time, Pallas kernels for 20%

profile of v1, /device:TPU:0, one launch (start us, length us, event | category | flops | bytes accessed | tf_op | source)
XLA Modules:
  0.0 154.0 jit_solution(11372346529361980483)
XLA Ops:
  1.0 3.6 %collective-permute-start.8 = (bf16[128,1024]{1,0:T(8,128)(2,1)}, bf16[128,1024]{1,0:T(8,128)(2,1)S(1)}, u32[]{:S(2)}, u32[]{:S(2)}) collective-permute-start(bf16[128,1024]{1,0:T(8,128)(2,1)} %refs_0_.1), channel_id=1, source_target_pairs={{0,2},{1,3},{2,0},{3,1},{4,6},{5,7},{6,4},{7,5},{8,10},{9,11},{10,... | collective-permute-start | bytes 786440 | tf_op jit(solution)/shard_map/ppermute | solution.py:209
  5.3 1.5 collective-permute-start.12
  6.8 2.1 %collective-permute-done.12 = f32[128,8]{0,1:T(8,128)S(1)} collective-permute-done((f32[128,8]{0,1:T(8,128)S(1)}, f32[128,8]{0,1:T(8,128)S(1)}, u32[]{:S(2)}, u32[]{:S(2)}) %collective-permute-start.12) | collective-permute-done | bytes 4128 | tf_op jit(solution)/shard_map/ppermute | solution.py:197
  8.9 1.5 collective-permute-start.11
  10.4 2.1 %collective-permute-done.11 = f32[128,8]{0,1:T(8,128)S(1)} collective-permute-done((f32[128,8]{0,1:T(8,128)S(1)}, f32[128,8]{0,1:T(8,128)S(1)}, u32[]{:S(2)}, u32[]{:S(2)}) %collective-permute-start.11) | collective-permute-done | bytes 4128 | tf_op jit(solution)/shard_map/ppermute | solution.py:197
  12.5 1.5 collective-permute-start.21
  14.0 2.1 %collective-permute-done.21 = f32[128,8]{0,1:T(8,128)S(1)} collective-permute-done((f32[128,8]{0,1:T(8,128)S(1)}, f32[128,8]{0,1:T(8,128)S(1)}, u32[]{:S(2)}, u32[]{:S(2)}) %collective-permute-start.21) | collective-permute-done | bytes 4128 | tf_op jit(solution)/shard_map/ppermute | solution.py:197
  16.1 1.6 %collective-permute-start.2 = (bf16[128,1024]{1,0:T(8,128)(2,1)}, bf16[128,1024]{1,0:T(8,128)(2,1)S(1)}, u32[]{:S(2)}, u32[]{:S(2)}) collective-permute-start(bf16[128,1024]{1,0:T(8,128)(2,1)} %refs_0_.1), channel_id=1, source_target_pairs={{0,1},{1,2},{2,3},{3,0},{4,5},{5,6},{6,7},{7,4},{8,9},{9,10},{10,1... | collective-permute-start | bytes 786440 | tf_op jit(solution)/shard_map/ppermute | solution.py:209
  17.7 3.3 %collective-permute-start.5 = (bf16[128,1024]{1,0:T(8,128)(2,1)}, bf16[128,1024]{1,0:T(8,128)(2,1)S(1)}, u32[]{:S(2)}, u32[]{:S(2)}) collective-permute-start(bf16[128,1024]{1,0:T(8,128)(2,1)} %refs_0_.1), channel_id=1, source_target_pairs={{0,3},{1,0},{2,1},{3,2},{4,7},{5,4},{6,5},{7,6},{8,11},{9,8},{10,9... | collective-permute-start | bytes 786440 | tf_op jit(solution)/shard_map/ppermute | solution.py:209
  21.0 5.9 %collective-permute-done.2.refs_3_ = bf16[128,1024]{1,0:T(8,128)(2,1)S(1)} collective-permute-done((bf16[128,1024]{1,0:T(8,128)(2,1)}, bf16[128,1024]{1,0:T(8,128)(2,1)S(1)}, u32[]{:S(2)}, u32[]{:S(2)}) %collective-permute-start.2) | collective-permute-done | bytes 262176 | tf_op jit(solution)/shard_map/ppermute | solution.py:209
  26.9 1.5 collective-permute-start.1
  28.4 1.1 collective-permute-done.5.refs_6_
  29.6 1.5 collective-permute-start
  31.1 3.7 %collective-permute-done.1.refs_2_ = bf16[128,1024]{1,0:T(8,128)(2,1)S(1)} collective-permute-done((bf16[128,1024]{1,0:T(8,128)(2,1)}, bf16[128,1024]{1,0:T(8,128)(2,1)S(1)}, u32[]{:S(2)}, u32[]{:S(2)}) %collective-permute-start.1) | collective-permute-done | bytes 262176 | tf_op jit(solution)/shard_map/ppermute | solution.py:197
  34.7 1.5 collective-permute-start.10
  36.3 2.6 %collective-permute-done.refs_1_ = bf16[128,1024]{1,0:T(8,128)(2,1)S(1)} collective-permute-done((bf16[128,1024]{1,0:T(8,128)(2,1)}, bf16[128,1024]{1,0:T(8,128)(2,1)S(1)}, u32[]{:S(2)}, u32[]{:S(2)}) %collective-permute-start) | collective-permute-done | bytes 262176 | tf_op jit(solution)/shard_map/ppermute | solution.py:197
  39.4 1.7 %collective-permute-done.10.refs_11_ = bf16[128,1024]{1,0:T(8,128)(2,1)S(1)} collective-permute-done((bf16[128,1024]{1,0:T(8,128)(2,1)S(1)}, bf16[128,1024]{1,0:T(8,128)(2,1)S(1)}, u32[]{:S(2)}, u32[]{:S(2)}) %collective-permute-start.10) | collective-permute-done | bytes 262176 | tf_op jit(solution)/shard_map/ppermute | solution.py:197
  41.1 1.5 collective-permute-start.7
  42.6 3.4 %collective-permute-done.4.refs_5_ = bf16[128,1024]{1,0:T(8,128)(2,1)S(1)} collective-permute-done((bf16[128,1024]{1,0:T(8,128)(2,1)S(1)}, bf16[128,1024]{1,0:T(8,128)(2,1)S(1)}, u32[]{:S(2)}, u32[]{:S(2)}) %collective-permute-start.4) | collective-permute-done | bytes 262176 | tf_op jit(solution)/shard_map/ppermute | solution.py:197
  46.1 1.5 collective-permute-start.3
  47.6 4.1 %collective-permute-done.7.refs_8_ = bf16[128,1024]{1,0:T(8,128)(2,1)S(1)} collective-permute-done((bf16[128,1024]{1,0:T(8,128)(2,1)S(1)}, bf16[128,1024]{1,0:T(8,128)(2,1)S(1)}, u32[]{:S(2)}, u32[]{:S(2)}) %collective-permute-start.7) | collective-permute-done | bytes 262176 | tf_op jit(solution)/shard_map/ppermute | solution.py:197
  51.7 1.5 collective-permute-start.6
  55.0 3.1 %collective-permute-done.6.refs_7_ = bf16[128,1024]{1,0:T(8,128)(2,1)S(1)} collective-permute-done((bf16[128,1024]{1,0:T(8,128)(2,1)S(1)}, bf16[128,1024]{1,0:T(8,128)(2,1)S(1)}, u32[]{:S(2)}, u32[]{:S(2)}) %collective-permute-start.6) | collective-permute-done | bytes 262176 | tf_op jit(solution)/shard_map/ppermute | solution.py:197
  58.8 1.5 collective-permute-start.17
  61.6 1.5 collective-permute-start.18
  63.6 1.5 collective-permute-start.20
  65.1 2.2 %copy-done = bf16[1,4096,512]{2,1,0:T(8,128)(2,1)S(1)} copy-done((bf16[1,4096,512]{2,1,0:T(8,128)(2,1)S(1)}, bf16[1,4096,512]{2,1,0:T(8,128)(2,1)}, u32[]{:S(2)}) %copy-start) | copy-done | bytes 4194328
  67.3 0.9 copy-done.3
  68.3 0.9 copy-done.5
  69.2 0.9 copy-done.7
  71.1 18.2 %shard_map.64 = (bf16[4,128,1024]{2,1,0:T(8,128)(2,1)S(1)}, bf16[4,128,1024]{2,1,0:T(8,128)(2,1)S(1)}, bf16[4,128,1024]{2,1,0:T(8,128)(2,1)S(1)}) custom-call(s32[1]{0:T(128)} %bitcast.place_ref, bf16[128,1024]{1,0:T(8,128)(2,1)S(1)} %copy-done.3, bf16[128,1024]{1,0:T(8,128)(2,1)S(1)} %collective-permute-done.refs_1_, ...), custom_call_target="tpu_custom_call" | custom-call | flops 9663676416 | bytes 31457280 | tf_op jit(solution)/shard_map/pallas_call | solution.py:156
  89.9 12.8 %shard_map.65 = (bf16[128,1024]{1,0:T(8,128)(2,1)S(1)}, bf16[128,1024]{1,0:T(8,128)(2,1)S(1)}, bf16[128,1024]{1,0:T(8,128)(2,1)S(1)}, bf16[128,1024]{1,0:T(8,128)(2,1)S(1)}) custom-call(s32[1]{0:T(128)} %bitcast.place_ref, bf16[128,1024]{1,0:T(8,128)(2,1)S(1)} %collective-permute-done.17.refs_0_, bf16[128,1024]{1,0:T(8,128)(2,1)S(1)} %collective-permute-done.18.refs_1_, ...), custom_call_target="tpu_custom_call" | custom-call | flops 3221225472 | bytes 27262976 | tf_op jit(solution)/shard_map/pallas_call | solution.py:156
  102.8 1.6 %collective-permute-start.22 = (bf16[128,1024]{1,0:T(8,128)(2,1)S(1)}, bf16[128,1024]{1,0:T(8,128)(2,1)S(1)}, u32[]{:S(2)}, u32[]{:S(2)}) collective-permute-start(bf16[128,1024]{1,0:T(8,128)(2,1)S(1)} %get-tuple-element.15), channel_id=1, source_target_pairs={{0,8},{4,20},{8,0},{12,28},{16,24},{20,4},{24,16},{28,12},{1,9},{5... | collective-permute-start | bytes 786440 | tf_op jit(solution)/shard_map/ppermute | solution.py:197
  104.9 1.5 collective-permute-start.27
  106.9 2.3 %collective-permute-done.22 = bf16[128,1024]{1,0:T(8,128)(2,1)S(1)} collective-permute-done((bf16[128,1024]{1,0:T(8,128)(2,1)S(1)}, bf16[128,1024]{1,0:T(8,128)(2,1)S(1)}, u32[]{:S(2)}, u32[]{:S(2)}) %collective-permute-start.22) | collective-permute-done | bytes 262176 | tf_op jit(solution)/shard_map/ppermute | solution.py:197
  109.2 2.8 %collective-permute-done.24 = bf16[128,1024]{1,0:T(8,128)(2,1)S(1)} collective-permute-done((bf16[128,1024]{1,0:T(8,128)(2,1)S(1)}, bf16[128,1024]{1,0:T(8,128)(2,1)S(1)}, u32[]{:S(2)}, u32[]{:S(2)}) %collective-permute-start.24) | collective-permute-done | bytes 262176 | tf_op jit(solution)/shard_map/ppermute | solution.py:197
  112.0 3.1 %collective-permute-done.27 = bf16[128,1024]{1,0:T(8,128)(2,1)S(1)} collective-permute-done((bf16[128,1024]{1,0:T(8,128)(2,1)S(1)}, bf16[128,1024]{1,0:T(8,128)(2,1)S(1)}, u32[]{:S(2)}, u32[]{:S(2)}) %collective-permute-start.27) | collective-permute-done | bytes 262176 | tf_op jit(solution)/shard_map/ppermute | solution.py:197
  115.1 5.6 %collective-permute-done.30 = bf16[128,1024]{1,0:T(8,128)(2,1)S(1)} collective-permute-done((bf16[128,1024]{1,0:T(8,128)(2,1)S(1)}, bf16[128,1024]{1,0:T(8,128)(2,1)S(1)}, u32[]{:S(2)}, u32[]{:S(2)}) %collective-permute-start.30) | collective-permute-done | bytes 262176 | tf_op jit(solution)/shard_map/ppermute | solution.py:197
  121.2 2.0 %collective-permute-start.28 = (bf16[128,1024]{1,0:T(8,128)(2,1)S(1)}, bf16[128,1024]{1,0:T(8,128)(2,1)S(1)}, u32[]{:S(2)}, u32[]{:S(2)}) collective-permute-start(bf16[128,1024]{1,0:T(8,128)(2,1)S(1)} %get-tuple-element.24), channel_id=1, source_target_pairs={{0,16},{4,12},{8,24},{12,4},{16,0},{20,28},{24,8},{28,20},{1,17},{... | collective-permute-start | bytes 786440 | tf_op jit(solution)/shard_map/ppermute | solution.py:197
  123.3 1.9 %collective-permute-start.23 = (bf16[128,1024]{1,0:T(8,128)(2,1)S(1)}, bf16[128,1024]{1,0:T(8,128)(2,1)S(1)}, u32[]{:S(2)}, u32[]{:S(2)}) collective-permute-start(bf16[128,1024]{1,0:T(8,128)(2,1)S(1)} %get-tuple-element.22), channel_id=1, source_target_pairs={{0,16},{4,12},{8,24},{12,4},{16,0},{20,28},{24,8},{28,20},{1,17},{... | collective-permute-start | bytes 786440 | tf_op jit(solution)/shard_map/ppermute | solution.py:197
  125.3 2.3 %collective-permute-done.25 = bf16[128,1024]{1,0:T(8,128)(2,1)S(1)} collective-permute-done((bf16[128,1024]{1,0:T(8,128)(2,1)S(1)}, bf16[128,1024]{1,0:T(8,128)(2,1)S(1)}, u32[]{:S(2)}, u32[]{:S(2)}) %collective-permute-start.25) | collective-permute-done | bytes 262176 | tf_op jit(solution)/shard_map/ppermute | solution.py:197
  127.6 2.8 %collective-permute-done.28 = bf16[128,1024]{1,0:T(8,128)(2,1)S(1)} collective-permute-done((bf16[128,1024]{1,0:T(8,128)(2,1)S(1)}, bf16[128,1024]{1,0:T(8,128)(2,1)S(1)}, u32[]{:S(2)}, u32[]{:S(2)}) %collective-permute-start.28) | collective-permute-done | bytes 262176 | tf_op jit(solution)/shard_map/ppermute | solution.py:197
  130.4 2.8 %collective-permute-done.31 = bf16[128,1024]{1,0:T(8,128)(2,1)S(1)} collective-permute-done((bf16[128,1024]{1,0:T(8,128)(2,1)S(1)}, bf16[128,1024]{1,0:T(8,128)(2,1)S(1)}, u32[]{:S(2)}, u32[]{:S(2)}) %collective-permute-start.31) | collective-permute-done | bytes 262176 | tf_op jit(solution)/shard_map/ppermute | solution.py:197
  133.7 7.5 %collective-permute-start.26 = (bf16[128,1024]{1,0:T(8,128)(2,1)S(1)}, bf16[128,1024]{1,0:T(8,128)(2,1)S(1)}, u32[]{:S(2)}, u32[]{:S(2)}) collective-permute-start(bf16[128,1024]{1,0:T(8,128)(2,1)S(1)} %get-tuple-element.19), channel_id=1, source_target_pairs={{0,2},{1,3},{2,0},{3,1},{4,6},{5,7},{6,4},{7,5},{8,10},{9,11},{10,... | collective-permute-start | bytes 786440 | tf_op jit(solution)/shard_map/ppermute | solution.py:209
  141.2 2.0 %collective-permute-start.32 = (bf16[128,1024]{1,0:T(8,128)(2,1)S(1)}, bf16[128,1024]{1,0:T(8,128)(2,1)S(1)}, u32[]{:S(2)}, u32[]{:S(2)}) collective-permute-start(bf16[128,1024]{1,0:T(8,128)(2,1)S(1)} %get-tuple-element.20), channel_id=1, source_target_pairs={{0,1},{1,2},{2,3},{3,0},{4,5},{5,6},{6,7},{7,4},{8,9},{9,10},{10,1... | collective-permute-start | bytes 786440 | tf_op jit(solution)/shard_map/ppermute | solution.py:209
  143.2 8.6 %collective-permute-done.26 = bf16[128,1024]{1,0:T(8,128)(2,1)S(1)} collective-permute-done((bf16[128,1024]{1,0:T(8,128)(2,1)S(1)}, bf16[128,1024]{1,0:T(8,128)(2,1)S(1)}, u32[]{:S(2)}, u32[]{:S(2)}) %collective-permute-start.26) | collective-permute-done | bytes 262176 | tf_op jit(solution)/shard_map/ppermute | solution.py:209
  151.8 1.2 collective-permute-done.29
  153.0 1.0 fusion.10
  (51 shorter events, 10.1 us)
Async XLA Ops:
  0.0 63.1 %collective-permute-start.13 = (bf16[4096,512]{1,0:T(8,128)(2,1)}, bf16[4096,512]{1,0:T(8,128)(2,1)}, u32[]{:S(2)}, u32[]{:S(2)}) collective-permute-start(bf16[4096,512]{1,0:T(8,128)(2,1)} %bitcast.38), channel_id=1, source_target_pairs={{0,4},{4,0},{8,12},{12,8},{16,20},{20,16},{24,28},{28,24},{1,5},{5... | collective-permute-start | bytes 12582920 | tf_op jit(solution)/shard_map/ppermute | solution.py:206
  0.5 63.2 %collective-permute-start.14 = (bf16[4096,512]{1,0:T(8,128)(2,1)}, bf16[4096,512]{1,0:T(8,128)(2,1)}, u32[]{:S(2)}, u32[]{:S(2)}) collective-permute-start(bf16[4096,512]{1,0:T(8,128)(2,1)} %bitcast.41), channel_id=1, source_target_pairs={{0,4},{4,0},{8,12},{12,8},{16,20},{20,16},{24,28},{28,24},{1,5},{5... | collective-permute-start | bytes 12582920 | tf_op jit(solution)/shard_map/ppermute | solution.py:206
  0.5 64.6 %collective-permute-start.15 = (bf16[512,4096]{1,0:T(8,128)(2,1)}, bf16[512,4096]{1,0:T(8,128)(2,1)}, u32[]{:S(2)}, u32[]{:S(2)}) collective-permute-start(bf16[512,4096]{1,0:T(8,128)(2,1)} %bitcast.44), channel_id=1, source_target_pairs={{0,4},{4,0},{8,12},{12,8},{16,20},{20,16},{24,28},{28,24},{1,5},{5... | collective-permute-start | bytes 12582920 | tf_op jit(solution)/shard_map/ppermute | solution.py:206
  1.0 16.7 %collective-permute-start.8 = (bf16[128,1024]{1,0:T(8,128)(2,1)}, bf16[128,1024]{1,0:T(8,128)(2,1)S(1)}, u32[]{:S(2)}, u32[]{:S(2)}) collective-permute-start(bf16[128,1024]{1,0:T(8,128)(2,1)} %refs_0_.1), channel_id=1, source_target_pairs={{0,2},{1,3},{2,0},{3,1},{4,6},{5,7},{6,4},{7,5},{8,10},{9,11},{10,... | collective-permute-start | bytes 786440 | tf_op jit(solution)/shard_map/ppermute | solution.py:209
  5.3 3.6 %collective-permute-start.12 = (f32[128,8]{0,1:T(8,128)S(1)}, f32[128,8]{0,1:T(8,128)S(1)}, u32[]{:S(2)}, u32[]{:S(2)}) collective-permute-start(f32[128,8]{0,1:T(8,128)S(1)} %select_reduce_fusion), channel_id=1, source_target_pairs={{0,16},{4,12},{8,24},{12,4},{16,0},{20,28},{24,8},{28,20},{1,17},{... | collective-permute-start | bytes 12296 | tf_op jit(solution)/shard_map/ppermute | solution.py:197
  8.9 3.6 %collective-permute-start.11 = (f32[128,8]{0,1:T(8,128)S(1)}, f32[128,8]{0,1:T(8,128)S(1)}, u32[]{:S(2)}, u32[]{:S(2)}) collective-permute-start(f32[128,8]{0,1:T(8,128)S(1)} %select_reduce_fusion), channel_id=1, source_target_pairs={{0,8},{4,20},{8,0},{12,28},{16,24},{20,4},{24,16},{28,12},{1,9},{5... | collective-permute-start | bytes 12296 | tf_op jit(solution)/shard_map/ppermute | solution.py:197
  12.5 3.6 %collective-permute-start.21 = (f32[128,8]{0,1:T(8,128)S(1)}, f32[128,8]{0,1:T(8,128)S(1)}, u32[]{:S(2)}, u32[]{:S(2)}) collective-permute-start(f32[128,8]{0,1:T(8,128)S(1)} %collective-permute-done.12), channel_id=1, source_target_pairs={{0,8},{4,20},{8,0},{12,28},{16,24},{20,4},{24,16},{28,12},{1,9},{5... | collective-permute-start | bytes 12296 | tf_op jit(solution)/shard_map/ppermute | solution.py:197
  16.1 10.9 %collective-permute-start.2 = (bf16[128,1024]{1,0:T(8,128)(2,1)}, bf16[128,1024]{1,0:T(8,128)(2,1)S(1)}, u32[]{:S(2)}, u32[]{:S(2)}) collective-permute-start(bf16[128,1024]{1,0:T(8,128)(2,1)} %refs_0_.1), channel_id=1, source_target_pairs={{0,1},{1,2},{2,3},{3,0},{4,5},{5,6},{6,7},{7,4},{8,9},{9,10},{10,1... | collective-permute-start | bytes 786440 | tf_op jit(solution)/shard_map/ppermute | solution.py:209
  17.7 11.9 %collective-permute-start.5 = (bf16[128,1024]{1,0:T(8,128)(2,1)}, bf16[128,1024]{1,0:T(8,128)(2,1)S(1)}, u32[]{:S(2)}, u32[]{:S(2)}) collective-permute-start(bf16[128,1024]{1,0:T(8,128)(2,1)} %refs_0_.1), channel_id=1, source_target_pairs={{0,3},{1,0},{2,1},{3,2},{4,7},{5,4},{6,5},{7,6},{8,11},{9,8},{10,9... | collective-permute-start | bytes 786440 | tf_op jit(solution)/shard_map/ppermute | solution.py:209
  26.9 7.8 %collective-permute-start.1 = (bf16[128,1024]{1,0:T(8,128)(2,1)}, bf16[128,1024]{1,0:T(8,128)(2,1)S(1)}, u32[]{:S(2)}, u32[]{:S(2)}) collective-permute-start(bf16[128,1024]{1,0:T(8,128)(2,1)} %refs_0_.1), channel_id=1, source_target_pairs={{0,16},{4,12},{8,24},{12,4},{16,0},{20,28},{24,8},{28,20},{1,17},{... | collective-permute-start | bytes 786440 | tf_op jit(solution)/shard_map/ppermute | solution.py:197
  29.6 9.3 %collective-permute-start = (bf16[128,1024]{1,0:T(8,128)(2,1)}, bf16[128,1024]{1,0:T(8,128)(2,1)S(1)}, u32[]{:S(2)}, u32[]{:S(2)}) collective-permute-start(bf16[128,1024]{1,0:T(8,128)(2,1)} %refs_0_.1), channel_id=1, source_target_pairs={{0,8},{4,20},{8,0},{12,28},{16,24},{20,4},{24,16},{28,12},{1,9},{5... | collective-permute-start | bytes 786440 | tf_op jit(solution)/shard_map/ppermute | solution.py:197
  34.7 6.4 %collective-permute-start.10 = (bf16[128,1024]{1,0:T(8,128)(2,1)S(1)}, bf16[128,1024]{1,0:T(8,128)(2,1)S(1)}, u32[]{:S(2)}, u32[]{:S(2)}) collective-permute-start(bf16[128,1024]{1,0:T(8,128)(2,1)S(1)} %collective-permute-done.8.refs_9_), channel_id=1, source_target_pairs={{0,16},{4,12},{8,24},{12,4},{16,0},{20,28},{24,8},{28,20},{1,17},{... | collective-permute-start | bytes 786440 | tf_op jit(solution)/shard_map/ppermute | solution.py:197
  38.9 7.2 %collective-permute-start.4 = (bf16[128,1024]{1,0:T(8,128)(2,1)S(1)}, bf16[128,1024]{1,0:T(8,128)(2,1)S(1)}, u32[]{:S(2)}, u32[]{:S(2)}) collective-permute-start(bf16[128,1024]{1,0:T(8,128)(2,1)S(1)} %collective-permute-done.2.refs_3_), channel_id=1, source_target_pairs={{0,16},{4,12},{8,24},{12,4},{16,0},{20,28},{24,8},{28,20},{1,17},{... | collective-permute-start | bytes 786440 | tf_op jit(solution)/shard_map/ppermute | solution.py:197
  41.1 10.6 %collective-permute-start.7 = (bf16[128,1024]{1,0:T(8,128)(2,1)S(1)}, bf16[128,1024]{1,0:T(8,128)(2,1)S(1)}, u32[]{:S(2)}, u32[]{:S(2)}) collective-permute-start(bf16[128,1024]{1,0:T(8,128)(2,1)S(1)} %collective-permute-done.5.refs_6_), channel_id=1, source_target_pairs={{0,16},{4,12},{8,24},{12,4},{16,0},{20,28},{24,8},{28,20},{1,17},{... | collective-permute-start | bytes 786440 | tf_op jit(solution)/shard_map/ppermute | solution.py:197
  46.1 7.1 %collective-permute-start.3 = (bf16[128,1024]{1,0:T(8,128)(2,1)S(1)}, bf16[128,1024]{1,0:T(8,128)(2,1)S(1)}, u32[]{:S(2)}, u32[]{:S(2)}) collective-permute-start(bf16[128,1024]{1,0:T(8,128)(2,1)S(1)} %collective-permute-done.2.refs_3_), channel_id=1, source_target_pairs={{0,8},{4,20},{8,0},{12,28},{16,24},{20,4},{24,16},{28,12},{1,9},{5... | collective-permute-start | bytes 786440 | tf_op jit(solution)/shard_map/ppermute | solution.py:197
  51.7 6.4 %collective-permute-start.6 = (bf16[128,1024]{1,0:T(8,128)(2,1)S(1)}, bf16[128,1024]{1,0:T(8,128)(2,1)S(1)}, u32[]{:S(2)}, u32[]{:S(2)}) collective-permute-start(bf16[128,1024]{1,0:T(8,128)(2,1)S(1)} %collective-permute-done.5.refs_6_), channel_id=1, source_target_pairs={{0,8},{4,20},{8,0},{12,28},{16,24},{20,4},{24,16},{28,12},{1,9},{5... | collective-permute-start | bytes 786440 | tf_op jit(solution)/shard_map/ppermute | solution.py:197
  53.2 0.7 copy-start.4
  53.9 7.0 %collective-permute-start.9 = (bf16[128,1024]{1,0:T(8,128)(2,1)S(1)}, bf16[128,1024]{1,0:T(8,128)(2,1)S(1)}, u32[]{:S(2)}, u32[]{:S(2)}) collective-permute-start(bf16[128,1024]{1,0:T(8,128)(2,1)S(1)} %collective-permute-done.8.refs_9_), channel_id=1, source_target_pairs={{0,8},{4,20},{8,0},{12,28},{16,24},{20,4},{24,16},{28,12},{1,9},{5... | collective-permute-start | bytes 786440 | tf_op jit(solution)/shard_map/ppermute | solution.py:197
  58.1 0.7 copy-start.6
  58.8 31.1 %collective-permute-start.17 = (bf16[128,1024]{1,0:T(8,128)(2,1)S(1)}, bf16[128,1024]{1,0:T(8,128)(2,1)S(1)}, u32[]{:S(2)}, u32[]{:S(2)}) collective-permute-start(bf16[128,1024]{1,0:T(8,128)(2,1)S(1)} %collective-permute-done.1.refs_2_), channel_id=1, source_target_pairs={{0,8},{4,20},{8,0},{12,28},{16,24},{20,4},{24,16},{28,12},{1,9},{5... | collective-permute-start | bytes 786440 | tf_op jit(solution)/shard_map/ppermute | solution.py:197
  60.9 0.7 copy-start.8
  61.6 28.3 %collective-permute-start.18 = (bf16[128,1024]{1,0:T(8,128)(2,1)S(1)}, bf16[128,1024]{1,0:T(8,128)(2,1)S(1)}, u32[]{:S(2)}, u32[]{:S(2)}) collective-permute-start(bf16[128,1024]{1,0:T(8,128)(2,1)S(1)} %collective-permute-done.4.refs_5_), channel_id=1, source_target_pairs={{0,8},{4,20},{8,0},{12,28},{16,24},{20,4},{24,16},{28,12},{1,9},{5... | collective-permute-start | bytes 786440 | tf_op jit(solution)/shard_map/ppermute | solution.py:197
  63.1 26.8 %collective-permute-start.19 = (bf16[128,1024]{1,0:T(8,128)(2,1)S(1)}, bf16[128,1024]{1,0:T(8,128)(2,1)S(1)}, u32[]{:S(2)}, u32[]{:S(2)}) collective-permute-start(bf16[128,1024]{1,0:T(8,128)(2,1)S(1)} %collective-permute-done.7.refs_8_), channel_id=1, source_target_pairs={{0,8},{4,20},{8,0},{12,28},{16,24},{20,4},{24,16},{28,12},{1,9},{5... | collective-permute-start | bytes 786440 | tf_op jit(solution)/shard_map/ppermute | solution.py:197
  63.6 26.3 %collective-permute-start.20 = (bf16[128,1024]{1,0:T(8,128)(2,1)S(1)}, bf16[128,1024]{1,0:T(8,128)(2,1)S(1)}, u32[]{:S(2)}, u32[]{:S(2)}) collective-permute-start(bf16[128,1024]{1,0:T(8,128)(2,1)S(1)} %collective-permute-done.10.refs_11_), channel_id=1, source_target_pairs={{0,8},{4,20},{8,0},{12,28},{16,24},{20,4},{24,16},{28,12},{1,9},{5... | collective-permute-start | bytes 786440 | tf_op jit(solution)/shard_map/ppermute | solution.py:197
  65.1 2.2 %copy-start = (bf16[1,4096,512]{2,1,0:T(8,128)(2,1)S(1)}, bf16[1,4096,512]{2,1,0:T(8,128)(2,1)}, u32[]{:S(2)}) copy-start(bf16[1,4096,512]{2,1,0:T(8,128)(2,1)} %param.9) | copy-start | bytes 12582916
  67.3 0.9 copy-start.3
  68.3 0.9 copy-start.5
  69.2 0.9 copy-start.7
  70.2 0.9 copy-start.9
  71.1 18.8 %copy-start.1 = (bf16[1,4096,512]{2,1,0:T(8,128)(2,1)S(1)}, bf16[1,4096,512]{2,1,0:T(8,128)(2,1)}, u32[]{:S(2)}) copy-start(bf16[1,4096,512]{2,1,0:T(8,128)(2,1)} %param.9) | copy-start | bytes 12582916
  71.1 18.8 %copy-start.2 = (bf16[1,4096,512]{2,1,0:T(8,128)(2,1)S(1)}, bf16[1,4096,512]{2,1,0:T(8,128)(2,1)}, u32[]{:S(2)}) copy-start(bf16[1,4096,512]{2,1,0:T(8,128)(2,1)} %param.10) | copy-start | bytes 12582916
  89.3 43.9 %collective-permute-start.16 = (bf16[4,128,1024]{2,1,0:T(8,128)(2,1)S(1)}, bf16[4,128,1024]{2,1,0:T(8,128)(2,1)S(1)}, u32[]{:S(2)}, u32[]{:S(2)}) collective-permute-start(bf16[4,128,1024]{2,1,0:T(8,128)(2,1)S(1)} %get-tuple-element.13), channel_id=1, source_target_pairs={{0,8},{4,20},{8,0},{12,28},{16,24},{20,4},{24,16},{28,12},{1,9},{5... | collective-permute-start | bytes 3145736 | tf_op jit(solution)/shard_map/ppermute | solution.py:197
  102.8 6.4 %collective-permute-start.22 = (bf16[128,1024]{1,0:T(8,128)(2,1)S(1)}, bf16[128,1024]{1,0:T(8,128)(2,1)S(1)}, u32[]{:S(2)}, u32[]{:S(2)}) collective-permute-start(bf16[128,1024]{1,0:T(8,128)(2,1)S(1)} %get-tuple-element.15), channel_id=1, source_target_pairs={{0,8},{4,20},{8,0},{12,28},{16,24},{20,4},{24,16},{28,12},{1,9},{5... | collective-permute-start | bytes 786440 | tf_op jit(solution)/shard_map/ppermute | solution.py:197
  104.3 7.7 %collective-permute-start.24 = (bf16[128,1024]{1,0:T(8,128)(2,1)S(1)}, bf16[128,1024]{1,0:T(8,128)(2,1)S(1)}, u32[]{:S(2)}, u32[]{:S(2)}) collective-permute-start(bf16[128,1024]{1,0:T(8,128)(2,1)S(1)} %get-tuple-element.16), channel_id=1, source_target_pairs={{0,8},{4,20},{8,0},{12,28},{16,24},{20,4},{24,16},{28,12},{1,9},{5... | collective-permute-start | bytes 786440 | tf_op jit(solution)/shard_map/ppermute | solution.py:197
  104.9 10.3 %collective-permute-start.27 = (bf16[128,1024]{1,0:T(8,128)(2,1)S(1)}, bf16[128,1024]{1,0:T(8,128)(2,1)S(1)}, u32[]{:S(2)}, u32[]{:S(2)}) collective-permute-start(bf16[128,1024]{1,0:T(8,128)(2,1)S(1)} %get-tuple-element.17), channel_id=1, source_target_pairs={{0,8},{4,20},{8,0},{12,28},{16,24},{20,4},{24,16},{28,12},{1,9},{5... | collective-permute-start | bytes 786440 | tf_op jit(solution)/shard_map/ppermute | solution.py:197
  106.4 14.4 %collective-permute-start.30 = (bf16[128,1024]{1,0:T(8,128)(2,1)S(1)}, bf16[128,1024]{1,0:T(8,128)(2,1)S(1)}, u32[]{:S(2)}, u32[]{:S(2)}) collective-permute-start(bf16[128,1024]{1,0:T(8,128)(2,1)S(1)} %get-tuple-element.18), channel_id=1, source_target_pairs={{0,8},{4,20},{8,0},{12,28},{16,24},{20,4},{24,16},{28,12},{1,9},{5... | collective-permute-start | bytes 786440 | tf_op jit(solution)/shard_map/ppermute | solution.py:197
  121.2 6.4 %collective-permute-start.25 = (bf16[128,1024]{1,0:T(8,128)(2,1)S(1)}, bf16[128,1024]{1,0:T(8,128)(2,1)S(1)}, u32[]{:S(2)}, u32[]{:S(2)}) collective-permute-start(bf16[128,1024]{1,0:T(8,128)(2,1)S(1)} %get-tuple-element.25), channel_id=1, source_target_pairs={{0,16},{4,12},{8,24},{12,4},{16,0},{20,28},{24,8},{28,20},{1,17},{... | collective-permute-start | bytes 786440 | tf_op jit(solution)/shard_map/ppermute | solution.py:197
  121.2 9.2 %collective-permute-start.28 = (bf16[128,1024]{1,0:T(8,128)(2,1)S(1)}, bf16[128,1024]{1,0:T(8,128)(2,1)S(1)}, u32[]{:S(2)}, u32[]{:S(2)}) collective-permute-start(bf16[128,1024]{1,0:T(8,128)(2,1)S(1)} %get-tuple-element.24), channel_id=1, source_target_pairs={{0,16},{4,12},{8,24},{12,4},{16,0},{20,28},{24,8},{28,20},{1,17},{... | collective-permute-start | bytes 786440 | tf_op jit(solution)/shard_map/ppermute | solution.py:197
  123.3 10.0 %collective-permute-start.31 = (bf16[128,1024]{1,0:T(8,128)(2,1)S(1)}, bf16[128,1024]{1,0:T(8,128)(2,1)S(1)}, u32[]{:S(2)}, u32[]{:S(2)}) collective-permute-start(bf16[128,1024]{1,0:T(8,128)(2,1)S(1)} %get-tuple-element.23), channel_id=1, source_target_pairs={{0,16},{4,12},{8,24},{12,4},{16,0},{20,28},{24,8},{28,20},{1,17},{... | collective-permute-start | bytes 786440 | tf_op jit(solution)/shard_map/ppermute | solution.py:197
  123.3 19.9 %collective-permute-start.23 = (bf16[128,1024]{1,0:T(8,128)(2,1)S(1)}, bf16[128,1024]{1,0:T(8,128)(2,1)S(1)}, u32[]{:S(2)}, u32[]{:S(2)}) collective-permute-start(bf16[128,1024]{1,0:T(8,128)(2,1)S(1)} %get-tuple-element.22), channel_id=1, source_target_pairs={{0,16},{4,12},{8,24},{12,4},{16,0},{20,28},{24,8},{28,20},{1,17},{... | collective-permute-start | bytes 786440 | tf_op jit(solution)/shard_map/ppermute | solution.py:197
  133.7 18.1 %collective-permute-start.26 = (bf16[128,1024]{1,0:T(8,128)(2,1)S(1)}, bf16[128,1024]{1,0:T(8,128)(2,1)S(1)}, u32[]{:S(2)}, u32[]{:S(2)}) collective-permute-start(bf16[128,1024]{1,0:T(8,128)(2,1)S(1)} %get-tuple-element.19), channel_id=1, source_target_pairs={{0,2},{1,3},{2,0},{3,1},{4,6},{5,7},{6,4},{7,5},{8,10},{9,11},{10,... | collective-permute-start | bytes 786440 | tf_op jit(solution)/shard_map/ppermute | solution.py:209
  141.2 11.8 %collective-permute-start.29 = (bf16[128,1024]{1,0:T(8,128)(2,1)S(1)}, bf16[128,1024]{1,0:T(8,128)(2,1)S(1)}, u32[]{:S(2)}, u32[]{:S(2)}) collective-permute-start(bf16[128,1024]{1,0:T(8,128)(2,1)S(1)} %get-tuple-element.21), channel_id=1, source_target_pairs={{0,3},{1,0},{2,1},{3,2},{4,7},{5,4},{6,5},{7,6},{8,11},{9,8},{10,9... | collective-permute-start | bytes 786440 | tf_op jit(solution)/shard_map/ppermute | solution.py:209
  141.2 11.8 %collective-permute-start.32 = (bf16[128,1024]{1,0:T(8,128)(2,1)S(1)}, bf16[128,1024]{1,0:T(8,128)(2,1)S(1)}, u32[]{:S(2)}, u32[]{:S(2)}) collective-permute-start(bf16[128,1024]{1,0:T(8,128)(2,1)S(1)} %get-tuple-element.20), channel_id=1, source_target_pairs={{0,1},{1,2},{2,3},{3,0},{4,5},{5,6},{6,7},{7,4},{8,9},{9,10},{10,1... | collective-permute-start | bytes 786440 | tf_op jit(solution)/shard_map/ppermute | solution.py:209
